TPU v7x, 32 devices: a whole 2x2x4 slice. The times are simulated.
32 devices in a mesh: groups: 2 (over y), cent: 4 (over z), pts: 4 (over x, core).
Axes of the slice: x: 2, y: 2, z: 4, core: 2. Of those that a mesh axis runs over, the one named last changes fastest.
Arguments:
- points: bfloat16 [4096, 1024], P(('groups', 'pts')), parts along dimension 0, may hold values from -12 to 12
- centres: bfloat16 [16384, 1024], P(('groups', 'cent')), parts along dimension 0, may hold values from -12 to 12
- alpha: float32 [16384], P(('groups', 'cent')), parts along dimension 0, may hold values from -30160460 to 30160460
Outputs:
- grads: float32 [4096, 1024], P(('groups', 'pts'), 'cent'), parts along dimension 0
- agop: float32 [2048, 1024], P(('groups', 'cent'), 'pts'), parts along dimension 0
There are 2 independent parts, one for each index of `groups`. A program takes and returns all parts, laid end to end along the dimension named above; each array names one. Nothing has to cross between parts.
All inputs are finite; a program needn't handle non-finite values.
Results may differ from a plain program's by a relative error of at most 0.002.
Values sent between devices are 32-bit elements; how exact they have to be, the bound alone decides.
A program may use at most 64 MiB of HBM per device.

v0:
```python
import jax
import jax.numpy as jnp
from jax import lax
from jax.sharding import PartitionSpec as P


def per_device(points, centres, alpha):
    width = points.shape[1]
    xf = points.astype(jnp.float32)
    zf = centres.astype(jnp.float32)
    pnorm = jnp.sum(xf * xf, axis=1)
    cross = jnp.dot(points, centres.T, preferred_element_type=jnp.float32)
    dist = pnorm[:, None] + jnp.sum(zf * zf, axis=1)[None, :] - 2.0 * cross
    weight = alpha[None, :] * jnp.exp(-2.0 * dist / width)
    wlow = weight.astype(jnp.bfloat16)
    partial_grad = (
        jnp.dot(wlow, centres, preferred_element_type=jnp.float32)
        - jnp.sum(weight, axis=1)[:, None] * xf
    )
    total_pts = points.shape[0] * lax.axis_size("pts")
    mine = lax.psum_scatter(partial_grad, "cent", scatter_dimension=1, tiled=True) * (4.0 / width)
    outer_rows = jnp.dot(
        mine.T,
        lax.all_gather(mine, "cent", axis=1, tiled=True),
        precision=lax.Precision.HIGHEST,
        preferred_element_type=jnp.float32,
    )
    agop = lax.psum_scatter(outer_rows, "pts", scatter_dimension=1, tiled=True) / total_pts
    return (mine, agop)


def solution(mesh):
    in_specs = (P(("groups", "pts"), None), P(("groups", "cent"), None), P(("groups", "cent")))
    out_specs = (P(("groups", "pts"), "cent"), P(("groups", "cent"), "pts"))
    return jax.shard_map(
        per_device, mesh=mesh, in_specs=in_specs, out_specs=out_specs, check_vma=False
    )
```

profile of v0, /device:TPU:1, one launch (start us, length us, event | category | flops | bytes accessed | tf_op | source)
XLA Modules:
  0.0 149.3 jit_solution(448164956107412834)
XLA Ops:
  7.2 0.0 copy-start.1
  7.2 0.0 copy-start.2
  7.2 0.0 reduce-scatter.3.cloned.1.call-start
  7.2 0.0 copy-start
  7.2 1.7 %fusion = f32[512]{0:T(512)S(1)} fusion(bf16[512,1024]{1,0:T(8,128)(2,1)} %param.3), kind=kLoop, calls=%fused_computation.4 | loop fusion | flops 1572352 | bytes 1050624 | tf_op jit(solution)/shard_map/reduce_sum | solution.py:11
  8.9 3.2 %multiply_reduce_fusion = f32[2048]{0:T(1024)S(1)} fusion(bf16[2048,1024]{1,0:T(8,128)(2,1)} %param.4), kind=kLoop, calls=%fused_computation | loop fusion | flops 6289408 | bytes 4202496 | tf_op jit(solution)/shard_map/reduce_sum | solution.py:13
  12.1 0.0 copy-done.1
  12.1 0.0 copy-done.2
  12.1 0.0 copy-done
  12.2 3.1 %fusion.6 = (f32[512]{0:T(512)S(1)}, bf16[512,2048]{1,0:T(8,128)(2,1)S(1)}) fusion(bf16[512,1024]{1,0:T(8,128)(2,1)S(1)} %copy-done.1, bf16[2048,1024]{1,0:T(8,128)(2,1)S(1)} %copy-done, f32[2048]{0:T(1024)S(1)} %multiply_reduce_fusion, f32[512]{0:T(512)S(1)} %fusion, f32[2048]{0:T(1024)S(1)} %copy-done.2), kind=kOutput, calls=%fused_computation.10 | convolution fusion | flops 2154823168 | bytes 7360512 | tf_op jit(solution)/shard_map/dot_general | solution.py:12
  15.3 3.7 %fusion.1 = f32[512,1024]{1,0:T(8,128)} fusion(bf16[512,1024]{1,0:T(8,128)(2,1)S(1)} %copy-done.1, bf16[2048,1024]{1,0:T(8,128)(2,1)S(1)} %copy-done, bf16[512,2048]{1,0:T(8,128)(2,1)S(1)} %get-tuple-element.3, f32[512]{0:T(512)S(1)} %get-tuple-element.2), kind=kOutput, calls=%fused_computation.5 | convolution fusion | flops 2149056512 | bytes 9439232 | tf_op jit(solution)/shard_map/dot_general | solution.py:17
  19.0 0.0 reduce-scatter.3.cloned.1.call-update
  19.0 0.0 all-gather.2.cloned.1.call-start
  19.1 45.9 %reduce-scatter.3.cloned.1.call-done = f32[512,256]{1,0:T(8,128)} async-done(((f32[512,1024]{1,0:T(8,128)}), f32[512,256]{1,0:T(8,128)}) %reduce-scatter.3.cloned.1.call-update) | async-done | bytes 524304 | tf_op jit(solution)/shard_map/reduce_scatter | solution.py:21
  65.0 1.9 %broadcast_multiply_fusion = f32[512,256]{1,0:T(8,128)} fusion(f32[512,256]{1,0:T(8,128)} %reduce-scatter.3.cloned.1.call-done), kind=kLoop, calls=%fused_computation.8 | loop fusion | flops 131072 | bytes 1048576 | tf_op jit(solution)/shard_map/mul | solution.py:21
  66.8 0.0 all-gather.2.cloned.1.call-update
  66.9 0.0 reduce-scatter.5.cloned.1.call-start
  66.9 45.7 %all-gather.2.cloned.1.call-done = f32[512,1024]{1,0:T(8,128)} async-done(((f32[512,256]{1,0:T(8,128)}), f32[512,1024]{1,0:T(8,128)}) %all-gather.2.cloned.1.call-update) | async-done | bytes 2097168 | tf_op jit(solution)/shard_map/all_gather | solution.py:24
  112.6 4.6 %fusion.7 = f32[256,1024]{1,0:T(8,128)} fusion(f32[512,256]{1,0:T(8,128)} %broadcast_multiply_fusion, f32[512,1024]{1,0:T(8,128)} %all-gather.2.cloned.1.call-done), kind=kOutput, calls=%fused_computation.11 | convolution fusion | flops 1610612736 | bytes 3670016 | tf_op jit(solution)/shard_map/dot_general | solution.py:22
  117.2 0.0 reduce-scatter.5.cloned.1.call-update
  117.2 23.8 %reduce-scatter.5.cloned.1.call-done = f32[256,256]{1,0:T(8,128)} async-done(((f32[256,1024]{1,0:T(8,128)}), f32[256,256]{1,0:T(8,128)}) %reduce-scatter.5.cloned.1.call-update) | async-done | bytes 262160 | tf_op jit(solution)/shard_map/reduce_scatter | solution.py:28
  141.1 1.7 %broadcast_multiply_fusion.1 = f32[256,256]{1,0:T(8,128)} fusion(f32[256,256]{1,0:T(8,128)} %reduce-scatter.5.cloned.1.call-done), kind=kLoop, calls=%fused_computation.9 | loop fusion | flops 65536 | bytes 524288 | tf_op jit(solution)/shard_map/div | solution.py:28
Async XLA Ops:
  7.2 5.0 %copy-start.1 = (bf16[512,1024]{1,0:T(8,128)(2,1)S(1)}, bf16[512,1024]{1,0:T(8,128)(2,1)}, u32[]{:S(2)}) copy-start(bf16[512,1024]{1,0:T(8,128)(2,1)} %param.3) | copy-start | bytes 3145732
  7.2 5.0 %copy-start.2 = (f32[2048]{0:T(1024)S(1)}, f32[2048]{0:T(1024)}, u32[]{:S(2)}) copy-start(f32[2048]{0:T(1024)} %param.5) | copy-start | bytes 24580
  7.2 57.8 %reduce-scatter.3.cloned.1.call-start = ((), (), s32[]{:S(2)}) async-start(), calls=%async_computation.2 | async-start | bytes 2621440 | tf_op jit(solution)/shard_map/reduce_scatter | solution.py:21
  7.2 4.9 %copy-start = (bf16[2048,1024]{1,0:T(8,128)(2,1)S(1)}, bf16[2048,1024]{1,0:T(8,128)(2,1)}, u32[]{:S(2)}) copy-start(bf16[2048,1024]{1,0:T(8,128)(2,1)} %param.4) | copy-start | bytes 12582916
  19.0 93.6 %all-gather.2.cloned.1.call-start = ((), (), s32[]{:S(2)}) async-start(), calls=%async_computation.3 | async-start | bytes 2621440 | tf_op jit(solution)/shard_map/all_gather | solution.py:24
  66.9 74.2 %reduce-scatter.5.cloned.1.call-start = ((), (), s32[]{:S(2)}) async-start(), calls=%async_computation.4 | async-start | bytes 1310720 | tf_op jit(solution)/shard_map/reduce_scatter | solution.py:28
Sparse Core Ops, SparseCore 0:
  19.1 45.7 reduce-scatter.2
  67.2 45.3 all-gather.1
  117.4 23.6 reduce-scatter.4
where the time goes:
time: 150 us; the launch traced here: 149 us
  waiting for transfers between devices  115 us (77%)
  between operations  13.8 us (9%)
  matrix products  11.5 us (8%)
  other arithmetic  8.42 us (6%)
    reduce_scatter x1, waiting for transfers between devices, per_device(): lax.psum_scatter(partial_grad, 'cent', scatter_dimension=1, tiled=True)  45.9 us
    all_gather x1, waiting for transfers between devices, per_device(): lax.all_gather(mine, 'cent', axis=1, tiled=True)  45.7 us
    reduce_scatter x1, waiting for transfers between devices, per_device(): lax.psum_scatter(outer_rows, 'pts', scatter_dimension=1, tiled=True)  23.8 us
    dot_general x1, matrix products, per_device(): jnp.dot(mine.T, lax.all_gather(mine, 'cent', axis=1, tiled=True), precisi...  4.61 us
    dot_general x1, matrix products, per_device(): jnp.dot(wlow, centres, preferred_element_type=jnp.float32)  3.74 us
    reduce_sum x1, other arithmetic, per_device(): dist = pnorm[:, None] + jnp.sum(zf * zf, axis=1)[None, :] - 2.0 * cross  3.23 us
    dot_general x1, matrix products, per_device(): cross = jnp.dot(points, centres.T, preferred_element_type=jnp.float32)  3.1 us
  transfers between devices with their start and end apart: 3, of which 3 were waited for; matrix products, arithmetic and copies ran while one was open for 0% of the time, Pallas kernels for 0%

commit v1 on v0

--- a/solution.py
+++ b/solution.py
@@ -1,10 +1,257 @@
+import functools
+
 import jax
 import jax.numpy as jnp
 from jax import lax
+from jax.experimental import pallas as pl
+from jax.experimental.pallas import tpu as pltpu
 from jax.sharding import PartitionSpec as P
 
-
-def per_device(points, centres, alpha):
+MESH = pl.DeviceIdType.MESH
+PIECES = 4
+GROUP = 2
+TILE = 512
+
+
+def kernel(n, total_pts, x_ref, z_ref, alpha_ref, grads_ref, agop_ref,
+           part, from_left, from_right, gall, acc, cnorm, wlow, t_core, t_own, t_x,
+           send_r, send_l, recv_r, recv_l, gsend_r, gsend_l, grecv, tsend, trecv, *, pieces):
+    me = lax.axis_index("cent")
+    p = lax.axis_index("pts")
+    chip, core = p // 2, lax.rem(p, 2)
+    rows, width = x_ref.shape
+    centres = z_ref.shape[0]
+    rb = rows // pieces
+    cols = width // n
+    right = {"cent": jnp.minimum(me + 1, n - 1)}
+    left = {"cent": jnp.maximum(me - 1, 0)}
+    other_core = {"pts": chip * 2 + 1 - core}
+    other_chip = {"pts": (1 - chip) * 2 + core}
+    has_left, has_right = me > 0, me < n - 1
+
+    def copy(src, dst, send, recv, target):
+        return pltpu.make_async_remote_copy(
+            src_ref=src, dst_ref=dst, send_sem=send, recv_sem=recv,
+            device_id=target, device_id_type=MESH)
+
+    def sum_r(r, d):
+        return copy(part.at[r, d], from_left.at[r, d], send_r.at[r, d], recv_r.at[r, d], right)
+
+    def sum_l(r, d):
+        return copy(part.at[r, d], from_right.at[r, d], send_l.at[r, d], recv_l.at[r, d], left)
+
+    def gather_r(r, s):
+        return copy(gall.at[r, s], gall.at[r, s], gsend_r.at[r, s], grecv.at[r, s], right)
+
+    def gather_l(r, s):
+        return copy(gall.at[r, s], gall.at[r, s], gsend_l.at[r, s], grecv.at[r, s], left)
+
+    barrier = pltpu.get_barrier_semaphore()
+
+    @pl.when(has_left)
+    def _():
+        pl.semaphore_signal(barrier, inc=1, device_id=left, device_id_type=MESH)
+
+    @pl.when(has_right)
+    def _():
+        pl.semaphore_signal(barrier, inc=1, device_id=right, device_id_type=MESH)
+
+    pl.semaphore_signal(barrier, inc=1, device_id=other_core, device_id_type=MESH)
+    pl.semaphore_signal(barrier, inc=1, device_id=other_chip, device_id_type=MESH)
+
+    @pl.loop(0, centres // 128)
+    def _(i):
+        at = pl.ds(pl.multiple_of(i * 128, 128), 128)
+        zf = z_ref[at, :].astype(jnp.float32)
+        sq = zf * zf
+        lanes = sq[:, 0:128]
+        for k in range(1, width // 128):
+            lanes = lanes + sq[:, k * 128:(k + 1) * 128]
+        cnorm[0:1, at] = jnp.sum(lanes.T, axis=0, keepdims=True)
+
+    acc[...] = jnp.zeros_like(acc)
+
+    def compute(g, waited):
+        gr = GROUP * rb
+        here = pl.ds(g * gr, gr)
+        xf = x_ref[here, :].astype(jnp.float32)
+        pnorm = jnp.sum(xf * xf, axis=1, keepdims=True)
+
+        def tile(i, wsum):
+            at = pl.ds(pl.multiple_of(i * TILE, TILE), TILE)
+            cross = lax.dot_general(
+                x_ref[here, :], z_ref[at, :], (((1,), (1,)), ((), ())),
+                preferred_element_type=jnp.float32)
+            dist = pnorm + cnorm[0:1, at] - 2.0 * cross
+            weight = alpha_ref[0:1, at] * jnp.exp(dist * (-2.0 / width))
+            wlow[:, at] = weight.astype(jnp.bfloat16)
+            return wsum + jnp.sum(weight, axis=1, keepdims=True)
+
+        wsum = lax.fori_loop(0, centres // TILE, tile, jnp.zeros((gr, 1), jnp.float32))
+        if not waited:
+            pl.semaphore_wait(barrier, 2 + has_left.astype(jnp.int32) + has_right.astype(jnp.int32))
+
+        @pl.loop(0, n)
+        def _(k):
+            d = jnp.where(me * 2 < n, n - 1 - k, k)
+            at = pl.ds(pl.multiple_of(d * cols, cols), cols)
+            term = jnp.dot(wlow[...], z_ref[:, at], preferred_element_type=jnp.float32)
+            term = term - wsum * x_ref[here, at].astype(jnp.float32)
+            for j in range(GROUP):
+                r = g * GROUP + j
+                part[r, d] = term[j * rb:(j + 1) * rb]
+
+                @pl.when((me == 0) & (d > 0))
+                def _():
+                    sum_r(r, d).start()
+
+                @pl.when((me == n - 1) & (d < n - 1))
+                def _():
+                    sum_l(r, d).start()
+
+    def scatter(r):
+        for k in range(n):
+            d = n - 1 - k
+
+            @pl.when(has_left & (me < d))
+            def _():
+                sum_r(r, d).wait_recv()
+                part[r, d] = part[r, d] + from_left[r, d]
+                sum_r(r, d).start()
+
+            @pl.when(has_right & (me > k))
+            def _():
+                sum_l(r, k).wait_recv()
+                part[r, k] = part[r, k] + from_right[r, k]
+                sum_l(r, k).start()
+
+        @pl.when(has_left)
+        def _():
+            sum_r(r, me).wait_recv()
+            part[r, me] = part[r, me] + from_left[r, me]
+
+        @pl.when(has_right)
+        def _():
+            sum_l(r, me).wait_recv()
+            part[r, me] = part[r, me] + from_right[r, me]
+
+        mine = part[r, me] * (4.0 / width)
+        gall[r, me] = mine
+        grads_ref[r * rb:(r + 1) * rb, :] = mine
+
+        @pl.when(has_right)
+        def _():
+            gather_r(r, me).start()
+
+        @pl.when(has_left)
+        def _():
+            gather_l(r, me).start()
+
+    def gather(r):
+        for k in range(n):
+            s = n - 1 - k
+
+            @pl.when(me > s)
+            def _():
+                gather_r(r, s).wait_recv()
+
+                @pl.when(has_right)
+                def _():
+                    gather_r(r, s).start()
+
+            @pl.when(me < k)
+            def _():
+                gather_l(r, k).wait_recv()
+
+                @pl.when(has_left)
+                def _():
+                    gather_l(r, k).start()
+
+        @pl.loop(0, n)
+        def _(s):
+            acc[s] = acc[s] + lax.dot_general(
+                gall[r, me], gall[r, s], (((0,), (0,)), ((), ())),
+                precision=lax.Precision.HIGHEST, preferred_element_type=jnp.float32)
+
+    for g in range(pieces // GROUP):
+        compute(g, g > 0)
+    for r in range(pieces):
+        scatter(r)
+        if r > 0:
+            gather(r - 1)
+    gather(pieces - 1)
+
+    far, near = (1 - chip) * 2, chip * 2
+    one = copy(acc.at[far + 1 - core], t_core, tsend.at[0], trecv.at[0], other_core)
+    two = copy(acc.at[near + 1 - core], t_own, tsend.at[1], trecv.at[1], other_core)
+    three = copy(acc.at[far + core], t_x, tsend.at[2], trecv.at[2], other_chip)
+    one.start()
+    two.start()
+    one.wait_recv()
+    acc[far + core] = acc[far + core] + t_core[...]
+    three.start()
+    two.wait_recv()
+    own = acc[near + core] + t_own[...]
+    three.wait_recv()
+    agop_ref[...] = (own + t_x[...]) / total_pts
+
+    one.wait_send()
+    two.wait_send()
+    three.wait_send()
+    for r in range(pieces):
+        for d in range(n):
+            @pl.when(has_right & (me < d))
+            def _():
+                sum_r(r, d).wait_send()
+
+            @pl.when(has_left & (me > d))
+            def _():
+                sum_l(r, d).wait_send()
+
+            @pl.when(has_right & (me >= d))
+            def _():
+                gather_r(r, d).wait_send()
+
+            @pl.when(has_left & (me <= d))
+            def _():
+                gather_l(r, d).wait_send()
+
+
+def fused(n, total_pts, points, centres, alpha):
+    rows, width = points.shape
+    cols, cen = width // n, centres.shape[0]
+    rb = rows // PIECES
+    chunks = pltpu.VMEM((PIECES, n, rb, cols), jnp.float32)
+    block = pltpu.VMEM((cols, cols), jnp.float32)
+    sems = pltpu.SemaphoreType.DMA((PIECES, n))
+    vmem = pl.BlockSpec(memory_space=pltpu.VMEM)
+    return pl.pallas_call(
+        functools.partial(kernel, n, float(total_pts), pieces=PIECES),
+        out_shape=(
+            jax.ShapeDtypeStruct((rows, cols), jnp.float32),
+            jax.ShapeDtypeStruct((cols, cols), jnp.float32),
+        ),
+        in_specs=[vmem] * 3,
+        out_specs=(vmem, vmem),
+        scratch_shapes=[
+            chunks, chunks, chunks, chunks,
+            pltpu.VMEM((n, cols, cols), jnp.float32),
+            pltpu.VMEM((8, cen), jnp.float32),
+            pltpu.VMEM((GROUP * rb, cen), jnp.bfloat16),
+            block, block, block,
+            sems, sems, sems, sems, sems, sems, sems,
+            pltpu.SemaphoreType.DMA((3,)),
+            pltpu.SemaphoreType.DMA((3,)),
+        ],
+        compiler_params=pltpu.CompilerParams(
+            collective_id=0, has_side_effects=True, vmem_limit_bytes=48 * 1024 * 1024),
+        cost_estimate=pl.CostEstimate(
+            flops=4 * rows * width * cen, bytes_accessed=8 * 1024 * 1024,
+            transcendentals=rows * cen),
+    )(points, centres, alpha.reshape(1, cen))
+
+
+def plain(total_pts, points, centres, alpha):
     width = points.shape[1]
     xf = points.astype(jnp.float32)
     zf = centres.astype(jnp.float32)
@@ -17,7 +264,6 @@
         jnp.dot(wlow, centres, preferred_element_type=jnp.float32)
         - jnp.sum(weight, axis=1)[:, None] * xf
     )
-    total_pts = points.shape[0] * lax.axis_size("pts")
     mine = lax.psum_scatter(partial_grad, "cent", scatter_dimension=1, tiled=True) * (4.0 / width)
     outer_rows = jnp.dot(
         mine.T,
@@ -30,6 +276,17 @@
 
 
 def solution(mesh):
+    n, npts = mesh.shape["cent"], mesh.shape["pts"]
+
+    def per_device(points, centres, alpha):
+        rows, width = points.shape
+        total_pts = rows * npts
+        fits = (n == npts == 4 and width % (128 * n) == 0
+                and rows % (16 * PIECES) == 0 and centres.shape[0] % TILE == 0)
+        if fits:
+            return fused(n, total_pts, points, centres, alpha)
+        return plain(total_pts, points, centres, alpha)
+
     in_specs = (P(("groups", "pts"), None), P(("groups", "cent"), None), P(("groups", "cent")))
     out_specs = (P(("groups", "pts"), "cent"), P(("groups", "cent"), "pts"))
     return jax.shard_map(

time: 150 us -> 131 us (0.87)
  Pallas kernels: 0 us -> 125 us
  waiting for transfers between devices: 115 us -> 0 us
  between operations: 13.8 us -> 0.65 us
  matrix products: 11.5 us -> 0 us
  other arithmetic: 8.42 us -> 0 us
  local copies, waits for them, and re-layouts: 0.01 us -> 5.6 us
    pallas_call x0 -> x1, Pallas kernels: none -> 125 us  [fused(): pl.pallas_call(functools.partial(kernel, n, float(total_pts), pieces=PIEC...]
    reduce_scatter x2 -> x0, waiting for transfers between devices: 69.7 us -> none  [the longest x1 45.9 us: per_device(): lax.psum_scatter(partial_grad, 'cent', scatter_dimension=1, tiled=True)]
    all_gather x1 -> x0, waiting for transfers between devices: 45.7 us -> none  [per_device(): lax.all_gather(mine, 'cent', axis=1, tiled=True)]
    dot_general x3 -> x0, matrix products: 11.5 us -> none  [the longest x1 4.61 us: per_device(): jnp.dot(mine.T, lax.all_gather(mine, 'cent', axis=1, tiled=True), precisi...]
    unnamed x6 -> x8, local copies, waits for them, and re-layouts: 0.01 us -> 5.6 us
    reduce_sum x2 -> x0, other arithmetic: 4.88 us -> none  [the longest x1 3.23 us: per_device(): dist = pnorm[:, None] + jnp.sum(zf * zf, axis=1)[None, :] - 2.0 * cross]
    mul x1 -> x0, other arithmetic: 1.87 us -> none  [per_device(): lax.psum_scatter(partial_grad, 'cent', scatter_dimension=1, tiled=True)]
    div x1 -> x0, other arithmetic: 1.67 us -> none  [per_device(): lax.psum_scatter(outer_rows, 'pts', scatter_dimension=1, tiled=True)]
  transfers between devices with their start and end apart: 3 -> 0, of which waited for: 3 -> 0; matrix products, arithmetic and copies ran while one was open for 0% -> 0% of each run, Pallas kernels for 0% -> 0%
where the time goes in v1:
time: 131 us
  Pallas kernels  125 us (95%)
  local copies, waits for them, and re-layouts  5.6 us (4%)
    pallas_call x1, Pallas kernels, fused(): pl.pallas_call(functools.partial(kernel, n, float(total_pts), pieces=PIEC...  125 us
    unnamed x8, local copies, waits for them, and re-layouts  5.6 us

profile of v1, /device:TPU:1, one launch (start us, length us, event | category | flops | bytes accessed | tf_op | source)
XLA Modules:
  0.0 131.0 jit_solution(15877924433763676134)
XLA Ops:
  0.6 0.0 copy-start
  0.6 2.2 %copy-done = bf16[2048,1024]{1,0:T(8,128)(2,1)S(1)} copy-done((bf16[2048,1024]{1,0:T(8,128)(2,1)S(1)}, bf16[2048,1024]{1,0:T(8,128)(2,1)}, u32[]{:S(2)}) %copy-start) | copy-done | bytes 4194328
  2.8 0.0 copy-start.1
  2.8 1.2 copy-done.1
  4.0 0.0 copy-start.2
  4.0 0.7 copy-done.2
  4.7 124.8 %shard_map.50 = (f32[512,256]{1,0:T(8,128)S(1)}, f32[256,256]{1,0:T(8,128)S(1)}) custom-call(bf16[512,1024]{1,0:T(8,128)(2,1)S(1)} %copy-done.1, bf16[2048,1024]{1,0:T(8,128)(2,1)S(1)} %copy-done, f32[1,2048]{1,0:T(1,128)S(1)} %bitcast.1), custom_call_target="tpu_custom_call" | custom-call | flops 4294967296 | bytes 8388608 | tf_op jit(solution)/shard_map/pallas_call | solution.py:228
  129.5 0.8 copy.7
  130.3 0.7 copy.8
Async XLA Ops:
  0.6 2.2 %copy-start = (bf16[2048,1024]{1,0:T(8,128)(2,1)S(1)}, bf16[2048,1024]{1,0:T(8,128)(2,1)}, u32[]{:S(2)}) copy-start(bf16[2048,1024]{1,0:T(8,128)(2,1)} %z_ref.1) | copy-start | bytes 12582916
  2.8 1.2 copy-start.1
  4.0 0.7 copy-start.2

commit v2 on v1

--- a/solution.py
+++ b/solution.py
@@ -8,8 +8,10 @@
 from jax.sharding import PartitionSpec as P
 
 MESH = pl.DeviceIdType.MESH
-PIECES = 4
-GROUP = 2
+PIECES = 2
+GROUP = 1
+AHEAD = 2
+LAG = 1
 TILE = 512
 
 
@@ -71,6 +73,15 @@
 
     acc[...] = jnp.zeros_like(acc)
 
+    def begin(r, d):
+        @pl.when((me == 0) & (d > 0))
+        def _():
+            sum_r(r, d).start()
+
+        @pl.when((me == n - 1) & (d < n - 1))
+        def _():
+            sum_l(r, d).start()
+
     def compute(g, waited):
         gr = GROUP * rb
         here = pl.ds(g * gr, gr)
@@ -101,13 +112,8 @@
                 r = g * GROUP + j
                 part[r, d] = term[j * rb:(j + 1) * rb]
 
-                @pl.when((me == 0) & (d > 0))
-                def _():
-                    sum_r(r, d).start()
-
-                @pl.when((me == n - 1) & (d < n - 1))
-                def _():
-                    sum_l(r, d).start()
+                if r < AHEAD:
+                    begin(r, d)
 
     def scatter(r):
         for k in range(n):
@@ -167,19 +173,27 @@
                 def _():
                     gather_l(r, k).start()
 
+        if r % 2 == 0:
+            return
+        rows_me = gall[r - 1:r + 1, me].reshape(2 * rb, cols)
+
         @pl.loop(0, n)
         def _(s):
             acc[s] = acc[s] + lax.dot_general(
-                gall[r, me], gall[r, s], (((0,), (0,)), ((), ())),
+                rows_me, gall[r - 1:r + 1, s].reshape(2 * rb, cols), (((0,), (0,)), ((), ())),
                 precision=lax.Precision.HIGHEST, preferred_element_type=jnp.float32)
 
-    for g in range(pieces // GROUP):
-        compute(g, g > 0)
-    for r in range(pieces):
-        scatter(r)
-        if r > 0:
-            gather(r - 1)
-    gather(pieces - 1)
+    compute(0, False)
+    for r in range(pieces + LAG):
+        if r == 0:
+            compute(1, True)
+        if r < pieces:
+            scatter(r)
+            if r + AHEAD < pieces:
+                for k in range(n):
+                    begin(r + AHEAD, jnp.where(me == 0, n - 1 - k, k))
+        if r >= LAG:
+            gather(r - LAG)
 
     far, near = (1 - chip) * 2, chip * 2
     one = copy(acc.at[far + 1 - core], t_core, tsend.at[0], trecv.at[0], other_core)

time: 131 us -> 108 us (0.82)
  Pallas kernels: 125 us -> 102 us
    pallas_call x1, Pallas kernels: 125 us -> 102 us  [fused(): pl.pallas_call(functools.partial(kernel, n, float(total_pts), pieces=PIEC...]
where the time goes in v2:
time: 108 us
  Pallas kernels  102 us (94%)
  local copies, waits for them, and re-layouts  5.6 us (5%)
    pallas_call x1, Pallas kernels, fused(): pl.pallas_call(functools.partial(kernel, n, float(total_pts), pieces=PIEC...  102 us
    unnamed x8, local copies, waits for them, and re-layouts  5.6 us

profile of v2, /device:TPU:1, one launch (start us, length us, event | category | flops | bytes accessed | tf_op | source)
XLA Modules:
  0.0 108.0 jit_solution(10347487357160739704)
XLA Ops:
  0.6 0.0 copy-start
  0.6 2.2 %copy-done = bf16[2048,1024]{1,0:T(8,128)(2,1)S(1)} copy-done((bf16[2048,1024]{1,0:T(8,128)(2,1)S(1)}, bf16[2048,1024]{1,0:T(8,128)(2,1)}, u32[]{:S(2)}) %copy-start) | copy-done | bytes 4194328
  2.8 0.0 copy-start.1
  2.8 1.2 %copy-done.1 = bf16[512,1024]{1,0:T(8,128)(2,1)S(1)} copy-done((bf16[512,1024]{1,0:T(8,128)(2,1)S(1)}, bf16[512,1024]{1,0:T(8,128)(2,1)}, u32[]{:S(2)}) %copy-start.1) | copy-done | bytes 1048600
  4.0 0.0 copy-start.2
  4.0 0.7 copy-done.2
  4.7 101.7 %shard_map.50 = (f32[512,256]{1,0:T(8,128)S(1)}, f32[256,256]{1,0:T(8,128)S(1)}) custom-call(bf16[512,1024]{1,0:T(8,128)(2,1)S(1)} %copy-done.1, bf16[2048,1024]{1,0:T(8,128)(2,1)S(1)} %copy-done, f32[1,2048]{1,0:T(1,128)S(1)} %bitcast.1), custom_call_target="tpu_custom_call" | custom-call | flops 4294967296 | bytes 8388608 | tf_op jit(solution)/shard_map/pallas_call | solution.py:242
  106.5 0.8 copy.7
  107.3 0.7 copy.8
Async XLA Ops:
  0.6 2.2 %copy-start = (bf16[2048,1024]{1,0:T(8,128)(2,1)S(1)}, bf16[2048,1024]{1,0:T(8,128)(2,1)}, u32[]{:S(2)}) copy-start(bf16[2048,1024]{1,0:T(8,128)(2,1)} %z_ref.1) | copy-start | bytes 12582916
  2.8 1.2 %copy-start.1 = (bf16[512,1024]{1,0:T(8,128)(2,1)S(1)}, bf16[512,1024]{1,0:T(8,128)(2,1)}, u32[]{:S(2)}) copy-start(bf16[512,1024]{1,0:T(8,128)(2,1)} %x_ref.1) | copy-start | bytes 3145732
  4.0 0.7 copy-start.2

commit v3 on v2

--- a/solution.py
+++ b/solution.py
@@ -16,7 +16,7 @@
 
 
 def kernel(n, total_pts, x_ref, z_ref, alpha_ref, grads_ref, agop_ref,
-           part, from_left, from_right, gall, acc, cnorm, wlow, t_core, t_own, t_x,
+           part, from_left, from_right, gall, acc, cnorm, wlow, t_core, t_own, t_x, t_send, t_mirror,
            send_r, send_l, recv_r, recv_l, gsend_r, gsend_l, grecv, tsend, trecv, *, pieces):
     me = lax.axis_index("cent")
     p = lax.axis_index("pts")
@@ -28,8 +28,12 @@
     right = {"cent": jnp.minimum(me + 1, n - 1)}
     left = {"cent": jnp.maximum(me - 1, 0)}
     other_core = {"pts": chip * 2 + 1 - core}
+    mirror = {"cent": p, "pts": me}
     other_chip = {"pts": (1 - chip) * 2 + core}
     has_left, has_right = me > 0, me < n - 1
+
+    def here_made(s):
+        return (me == s) | (has_left & ((s == 0) | (s > me)))
 
     def copy(src, dst, send, recv, target):
         return pltpu.make_async_remote_copy(
@@ -60,6 +64,10 @@
 
     pl.semaphore_signal(barrier, inc=1, device_id=other_core, device_id_type=MESH)
     pl.semaphore_signal(barrier, inc=1, device_id=other_chip, device_id_type=MESH)
+
+    @pl.when(me != p)
+    def _():
+        pl.semaphore_signal(barrier, inc=1, device_id=mirror, device_id_type=MESH)
 
     @pl.loop(0, centres // 128)
     def _(i):
@@ -100,7 +108,8 @@
 
         wsum = lax.fori_loop(0, centres // TILE, tile, jnp.zeros((gr, 1), jnp.float32))
         if not waited:
-            pl.semaphore_wait(barrier, 2 + has_left.astype(jnp.int32) + has_right.astype(jnp.int32))
+            pl.semaphore_wait(barrier, 2 + has_left.astype(jnp.int32) + has_right.astype(jnp.int32)
+                              + (me != p).astype(jnp.int32))
 
         @pl.loop(0, n)
         def _(k):
@@ -145,31 +154,29 @@
         gall[r, me] = mine
         grads_ref[r * rb:(r + 1) * rb, :] = mine
 
-        @pl.when(has_right)
+        @pl.when(me == 0)
         def _():
             gather_r(r, me).start()
 
+        @pl.when(me > 1)
+        def _():
+            gather_l(r, me).start()
+
+    def gather(r):
         @pl.when(has_left)
         def _():
-            gather_l(r, me).start()
-
-    def gather(r):
-        for k in range(n):
-            s = n - 1 - k
-
-            @pl.when(me > s)
-            def _():
-                gather_r(r, s).wait_recv()
-
-                @pl.when(has_right)
-                def _():
-                    gather_r(r, s).start()
-
-            @pl.when(me < k)
+            gather_r(r, 0).wait_recv()
+
+            @pl.when(has_right)
+            def _():
+                gather_r(r, 0).start()
+
+        for k in range(2, n):
+            @pl.when(has_left & (me < k))
             def _():
                 gather_l(r, k).wait_recv()
 
-                @pl.when(has_left)
+                @pl.when(me > 1)
                 def _():
                     gather_l(r, k).start()
 
@@ -179,9 +186,11 @@
 
         @pl.loop(0, n)
         def _(s):
-            acc[s] = acc[s] + lax.dot_general(
-                rows_me, gall[r - 1:r + 1, s].reshape(2 * rb, cols), (((0,), (0,)), ((), ())),
-                precision=lax.Precision.HIGHEST, preferred_element_type=jnp.float32)
+            @pl.when(here_made(s))
+            def _():
+                acc[s] = acc[s] + lax.dot_general(
+                    rows_me, gall[r - 1:r + 1, s].reshape(2 * rb, cols), (((0,), (0,)), ((), ())),
+                    precision=lax.Precision.HIGHEST, preferred_element_type=jnp.float32)
 
     compute(0, False)
     for r in range(pieces + LAG):
@@ -199,19 +208,53 @@
     one = copy(acc.at[far + 1 - core], t_core, tsend.at[0], trecv.at[0], other_core)
     two = copy(acc.at[near + 1 - core], t_own, tsend.at[1], trecv.at[1], other_core)
     three = copy(acc.at[far + core], t_x, tsend.at[2], trecv.at[2], other_chip)
-    one.start()
-    two.start()
-    one.wait_recv()
-    acc[far + core] = acc[far + core] + t_core[...]
-    three.start()
-    two.wait_recv()
-    own = acc[near + core] + t_own[...]
-    three.wait_recv()
-    agop_ref[...] = (own + t_x[...]) / total_pts
-
-    one.wait_send()
-    two.wait_send()
-    three.wait_send()
+    four = copy(t_send, t_mirror, tsend.at[3], trecv.at[3], mirror)
+
+    @pl.when(here_made(far + 1 - core))
+    def _():
+        one.start()
+
+    @pl.when(here_made(near + 1 - core))
+    def _():
+        two.start()
+
+    @pl.when(here_made(far + core))
+    def _():
+        one.wait_recv()
+        acc[far + core] = acc[far + core] + t_core[...]
+        three.start()
+
+    @pl.when(here_made(p))
+    def _():
+        two.wait_recv()
+        own = acc[p] + t_own[...]
+        three.wait_recv()
+        own = (own + t_x[...]) / total_pts
+        agop_ref[...] = own
+
+        @pl.when(me != p)
+        def _():
+            t_send[...] = own.T
+            four.start()
+            four.wait_send()
+
+    @pl.when(jnp.logical_not(here_made(p)))
+    def _():
+        four.wait_recv()
+        agop_ref[...] = t_mirror[...]
+
+    @pl.when(here_made(far + 1 - core))
+    def _():
+        one.wait_send()
+
+    @pl.when(here_made(near + 1 - core))
+    def _():
+        two.wait_send()
+
+    @pl.when(here_made(far + core))
+    def _():
+        three.wait_send()
+
     for r in range(pieces):
         for d in range(n):
             @pl.when(has_right & (me < d))
@@ -222,11 +265,12 @@
             def _():
                 sum_l(r, d).wait_send()
 
-            @pl.when(has_right & (me >= d))
-            def _():
-                gather_r(r, d).wait_send()
-
-            @pl.when(has_left & (me <= d))
+            if d == 0:
+                @pl.when(has_right)
+                def _():
+                    gather_r(r, d).wait_send()
+
+            @pl.when((me > 1) & (me <= d))
             def _():
                 gather_l(r, d).wait_send()
 
@@ -252,10 +296,10 @@
             pltpu.VMEM((n, cols, cols), jnp.float32),
             pltpu.VMEM((8, cen), jnp.float32),
             pltpu.VMEM((GROUP * rb, cen), jnp.bfloat16),
-            block, block, block,
+            block, block, block, block, block,
             sems, sems, sems, sems, sems, sems, sems,
-            pltpu.SemaphoreType.DMA((3,)),
-            pltpu.SemaphoreType.DMA((3,)),
+            pltpu.SemaphoreType.DMA((4,)),
+            pltpu.SemaphoreType.DMA((4,)),
         ],
         compiler_params=pltpu.CompilerParams(
             collective_id=0, has_side_effects=True, vmem_limit_bytes=48 * 1024 * 1024),

time: 108 us -> 103 us (0.954)
  Pallas kernels: 102 us -> 95.9 us
    pallas_call x1, Pallas kernels: 102 us -> 95.9 us  [fused(): pl.pallas_call(functools.partial(kernel, n, float(total_pts), pieces=PIEC...]
where the time goes in v3:
time: 103 us; the launch traced here: 102 us
  Pallas kernels  95.9 us (93%)
  local copies, waits for them, and re-layouts  5.6 us (5%)
    pallas_call x1, Pallas kernels, fused(): pl.pallas_call(functools.partial(kernel, n, float(total_pts), pieces=PIEC...  95.9 us
    unnamed x8, local copies, waits for them, and re-layouts  5.6 us

profile of v3, /device:TPU:1, one launch (start us, length us, event | category | flops | bytes accessed | tf_op | source)
XLA Modules:
  0.0 102.1 jit_solution(12048083884688916684)
XLA Ops:
  0.6 0.0 copy-start
  0.6 2.2 %copy-done = bf16[2048,1024]{1,0:T(8,128)(2,1)S(1)} copy-done((bf16[2048,1024]{1,0:T(8,128)(2,1)S(1)}, bf16[2048,1024]{1,0:T(8,128)(2,1)}, u32[]{:S(2)}) %copy-start) | copy-done | bytes 4194328
  2.8 0.0 copy-start.1
  2.8 1.2 %copy-done.1 = bf16[512,1024]{1,0:T(8,128)(2,1)S(1)} copy-done((bf16[512,1024]{1,0:T(8,128)(2,1)S(1)}, bf16[512,1024]{1,0:T(8,128)(2,1)}, u32[]{:S(2)}) %copy-start.1) | copy-done | bytes 1048600
  4.0 0.0 copy-start.2
  4.0 0.7 copy-done.2
  4.7 95.9 %shard_map.50 = (f32[512,256]{1,0:T(8,128)S(1)}, f32[256,256]{1,0:T(8,128)S(1)}) custom-call(bf16[512,1024]{1,0:T(8,128)(2,1)S(1)} %copy-done.1, bf16[2048,1024]{1,0:T(8,128)(2,1)S(1)} %copy-done, f32[1,2048]{1,0:T(1,128)S(1)} %bitcast.1), custom_call_target="tpu_custom_call" | custom-call | flops 4294967296 | bytes 8388608 | tf_op jit(solution)/shard_map/pallas_call | solution.py:286
  100.6 0.8 copy.7
  101.4 0.7 copy.8
Async XLA Ops:
  0.6 2.2 %copy-start = (bf16[2048,1024]{1,0:T(8,128)(2,1)S(1)}, bf16[2048,1024]{1,0:T(8,128)(2,1)}, u32[]{:S(2)}) copy-start(bf16[2048,1024]{1,0:T(8,128)(2,1)} %z_ref.1) | copy-start | bytes 12582916
  2.8 1.2 %copy-start.1 = (bf16[512,1024]{1,0:T(8,128)(2,1)S(1)}, bf16[512,1024]{1,0:T(8,128)(2,1)}, u32[]{:S(2)}) copy-start(bf16[512,1024]{1,0:T(8,128)(2,1)} %x_ref.1) | copy-start | bytes 3145732
  4.0 0.7 copy-start.2

commit v4 on v3

--- a/solution.py
+++ b/solution.py
@@ -180,17 +180,22 @@
                 def _():
                     gather_l(r, k).start()
 
-        if r % 2 == 0:
-            return
-        rows_me = gall[r - 1:r + 1, me].reshape(2 * rb, cols)
+        def halves(value):
+            high = value.astype(jnp.bfloat16)
+            return high, (value - high.astype(jnp.float32)).astype(jnp.bfloat16)
+
+        def times(a, b):
+            return lax.dot_general(
+                a, b, (((0,), (0,)), ((), ())), preferred_element_type=jnp.float32)
+
+        high, low = halves(gall[r, me])
 
         @pl.loop(0, n)
         def _(s):
             @pl.when(here_made(s))
             def _():
-                acc[s] = acc[s] + lax.dot_general(
-                    rows_me, gall[r - 1:r + 1, s].reshape(2 * rb, cols), (((0,), (0,)), ((), ())),
-                    precision=lax.Precision.HIGHEST, preferred_element_type=jnp.float32)
+                top, rest = halves(gall[r, s])
+                acc[s] = acc[s] + (times(high, top) + (times(high, rest) + times(low, top)))
 
     compute(0, False)
     for r in range(pieces + LAG):

time: 103 us -> 103 us (level)
  no operation moved by 1% of the time
where the time goes in v4:
time: 103 us
  Pallas kernels  96.4 us (94%)
  local copies, waits for them, and re-layouts  5.6 us (5%)
    pallas_call x1, Pallas kernels, fused(): pl.pallas_call(functools.partial(kernel, n, float(total_pts), pieces=PIEC...  96.4 us
    unnamed x8, local copies, waits for them, and re-layouts  5.6 us

profile of v4, /device:TPU:1, one launch (start us, length us, event | category | flops | bytes accessed | tf_op | source)
XLA Modules:
  0.0 102.7 jit_solution(14084375727748394340)
XLA Ops:
  0.6 0.0 copy-start
  0.6 2.2 %copy-done = bf16[2048,1024]{1,0:T(8,128)(2,1)S(1)} copy-done((bf16[2048,1024]{1,0:T(8,128)(2,1)S(1)}, bf16[2048,1024]{1,0:T(8,128)(2,1)}, u32[]{:S(2)}) %copy-start) | copy-done | bytes 4194328
  2.8 0.0 copy-start.1
  2.8 1.2 %copy-done.1 = bf16[512,1024]{1,0:T(8,128)(2,1)S(1)} copy-done((bf16[512,1024]{1,0:T(8,128)(2,1)S(1)}, bf16[512,1024]{1,0:T(8,128)(2,1)}, u32[]{:S(2)}) %copy-start.1) | copy-done | bytes 1048600
  4.0 0.0 copy-start.2
  4.0 0.7 copy-done.2
  4.7 96.4 %shard_map.50 = (f32[512,256]{1,0:T(8,128)S(1)}, f32[256,256]{1,0:T(8,128)S(1)}) custom-call(bf16[512,1024]{1,0:T(8,128)(2,1)S(1)} %copy-done.1, bf16[2048,1024]{1,0:T(8,128)(2,1)S(1)} %copy-done, f32[1,2048]{1,0:T(1,128)S(1)} %bitcast.1), custom_call_target="tpu_custom_call" | custom-call | flops 4294967296 | bytes 8388608 | tf_op jit(solution)/shard_map/pallas_call | solution.py:291
  101.2 0.8 copy.7
  102.0 0.7 copy.8
Async XLA Ops:
  0.6 2.2 %copy-start = (bf16[2048,1024]{1,0:T(8,128)(2,1)S(1)}, bf16[2048,1024]{1,0:T(8,128)(2,1)}, u32[]{:S(2)}) copy-start(bf16[2048,1024]{1,0:T(8,128)(2,1)} %z_ref.1) | copy-start | bytes 12582916
  2.8 1.2 %copy-start.1 = (bf16[512,1024]{1,0:T(8,128)(2,1)S(1)}, bf16[512,1024]{1,0:T(8,128)(2,1)}, u32[]{:S(2)}) copy-start(bf16[512,1024]{1,0:T(8,128)(2,1)} %x_ref.1) | copy-start | bytes 3145732
  4.0 0.7 copy-start.2
